TPU v7x, 32 devices: a whole 2x2x4 slice. The times are simulated.
32 devices in a mesh: sta: 8 (over z, y), tile: 4 (over x, core).
Axes of the slice: x: 2, y: 2, z: 4, core: 2. Of those that a mesh axis runs over, the one named last changes fastest.
Arguments:
- traces: bfloat16 [1536, 1536], P('sta', 'tile'), may hold values from -6 to 6
- fir_taps: float32 [4, 64], replicated, may hold values from -0.75 to 0.75
- band_gain: float32 [4], replicated, may hold values from 0.5 to 2
- starts: int32 [1536, 4], P('sta'), may hold values from 0 to 1152
- delays: int32 [1536, 8192], P('sta', 'tile'), may hold values from 0 to 127
- visibility: int32 [1536, 4], P('sta'), may hold values from 0 to 1, as said below
Outputs:
- image: float32 [8192, 256], P(('tile', 'sta'))
Inputs may be any that keep to these rules, and one draw needn't show every extreme that they name: `visibility`: 1 where the station contributes to the tile's grid points, else 0; how many stations a tile uses may differ from tile to tile.
All inputs are finite; a program needn't handle non-finite values.
Results may differ from a plain program's by a relative error of at most 0.0051.
Values may be sent and summed in bfloat16 or wider, within the bound.
A program may use at most 64 MiB of HBM per device.

v0:
```python
import functools
import math

import jax
import jax.numpy as jnp
from jax import lax
from jax.experimental import pallas as pl
from jax.experimental.pallas import tpu as pltpu
from jax.sharding import PartitionSpec as P

TAPS = 64
D = 128
L = 256
WLEN = 384
LANES = 128
CHUNK = 8
MESH = pl.DeviceIdType.MESH


def window_kernel(starts_ref, gain_ref, traces_ref, taps_ref, vis_ref, win_ref, padded, held):
    sta, samp = traces_ref.shape
    bands = taps_ref.shape[0]
    padded[:, :LANES] = jnp.zeros((sta, LANES), jnp.float32)
    padded[:, LANES + samp :] = jnp.zeros((sta, LANES), jnp.float32)
    padded[:, LANES : LANES + samp] = traces_ref[...].astype(jnp.float32)

    def take(i, carry):
        for k in range(CHUNK):
            s = i * CHUNK + k
            first = starts_ref[s] + (LANES - TAPS)
            whole = first // LANES
            row = padded[pl.ds(s, 1), pl.ds(pl.multiple_of(whole * LANES, LANES), 5 * LANES)]
            row = pltpu.roll(row, 5 * LANES - (first - whole * LANES), 1)
            held[pl.ds(s, 1), :] = row[:, : 4 * LANES]
        return carry

    lax.fori_loop(0, sta // CHUNK, take, 0)

    tables = []
    for b in range(bands):
        rows = jnp.broadcast_to(taps_ref[b : b + 1, :], (2 * LANES, 2 * LANES))
        table = pltpu.roll(rows, 0, 1, stride=1, stride_axis=0)[:, :LANES]
        high = table.astype(jnp.bfloat16)
        rest = table - high.astype(jnp.float32)
        mid = rest.astype(jnp.bfloat16)
        low = (rest - mid.astype(jnp.float32)).astype(jnp.bfloat16)
        tables.append((high, mid, low))
    parts = []
    for j in range(WLEN // LANES):
        x = held[:, j * LANES : (j + 2) * LANES].astype(jnp.bfloat16)
        total = None
        for b in range(bands):
            filtered = None
            for table in reversed(tables[b]):
                term = jnp.dot(x, table, preferred_element_type=jnp.float32)
                filtered = term if filtered is None else filtered + term
            term = filtered * filtered * gain_ref[b]
            total = term if total is None else total + term
        parts.append(total.astype(jnp.bfloat16).astype(jnp.float32))
    mean = sum(jnp.sum(part, axis=1, keepdims=True) for part in parts) / WLEN
    vis = vis_ref[...]
    for j, part in enumerate(parts):
        out = ((part - mean) * vis).astype(jnp.bfloat16)
        win_ref[:, j * LANES : (j + 1) * LANES] = out.astype(jnp.float32)


def stack_kernel(n, delays_ref, win_ref, out_ref, hankel, total, sent, got, send_sem, recv_sem):
    sta = delays_ref.shape[0]
    block = out_ref.shape[1]
    me = lax.axis_index("sta")
    tile = lax.axis_index("tile")

    barrier = pltpu.get_barrier_semaphore()

    def greet(o, carry):
        pl.semaphore_signal(
            barrier, inc=1, device_id=(lax.rem(me + o, n), tile), device_id_type=MESH
        )
        return carry

    lax.fori_loop(1, n, greet, 0)

    def build(i, carry):
        for k in range(CHUNK):
            s = i * CHUNK + k
            rows = jnp.broadcast_to(win_ref[pl.ds(s, 1), :], (LANES, WLEN))
            rows = pltpu.roll(rows, WLEN - (LANES - 1), 1, stride=1, stride_axis=0)
            rows = rows[:, :L].astype(jnp.bfloat16)
            at = pl.ds(pl.multiple_of(s * D, D), D)
            for a in range(L // LANES):
                hankel[a * LANES : (a + 1) * LANES, at] = rows[:, a * LANES : (a + 1) * LANES]
        return carry

    lax.fori_loop(0, sta // CHUNK, build, 0)

    step = 16
    levels = [
        (lax.broadcasted_iota(jnp.int32, (step, block), 0) + k * step)
        .astype(jnp.float32)
        .astype(jnp.bfloat16)
        for k in range(D // step)
    ]
    one = jnp.ones((step, block), jnp.bfloat16)
    zero = jnp.zeros((step, block), jnp.bfloat16)

    def stack(owner):
        columns = pl.ds(pl.multiple_of(owner * block, block), block)
        total[...] = jnp.zeros_like(total)

        def add(c, carry):
            near = delays_ref[pl.ds(pl.multiple_of(c * CHUNK, CHUNK), CHUNK), columns].astype(
                jnp.float32
            )
            pieces = []
            for k in range(CHUNK):
                row = jnp.broadcast_to(near[k : k + 1, :], (step, block)).astype(jnp.bfloat16)
                pieces.extend(jnp.where(row == level, one, zero) for level in levels)
            onehot = jnp.concatenate(pieces, axis=0)
            depth = CHUNK * D
            lhs = hankel[:, pl.ds(pl.multiple_of(c * depth, depth), depth)]
            total[...] += jnp.dot(lhs, onehot, preferred_element_type=jnp.float32)
            return carry

        lax.fori_loop(0, sta // CHUNK, add, 0)

    def copy_of(o):
        return pltpu.make_async_remote_copy(
            src_ref=sent.at[o - 1],
            dst_ref=got.at[o - 1],
            send_sem=send_sem.at[o - 1],
            recv_sem=recv_sem.at[o - 1],
            device_id=(lax.rem(me + o, n), tile),
            device_id_type=MESH,
        )

    pl.semaphore_wait(barrier, n - 1)

    def send(o, carry):
        stack(lax.rem(me + o, n))
        sent[o - 1] = total[...].astype(jnp.bfloat16)
        copy_of(o).start()
        return carry

    lax.fori_loop(1, n, send, 0)
    stack(me)

    def collect(o, carry):
        copy_of(o).wait()
        total[...] += got[o - 1].astype(jnp.float32)
        return carry

    lax.fori_loop(1, n, collect, 0)
    out_ref[...] = total[...] * (1.0 / math.sqrt(sta * n))


def on_device(traces, fir_taps, band_gain, starts, delays, visibility):
    sta = traces.shape[0]
    n = lax.axis_size("sta")
    tile_pos = lax.axis_index("tile")
    gathered = lax.all_gather(traces, "tile", axis=1, tiled=True)
    begin_at = lax.dynamic_index_in_dim(starts, tile_pos, 1, keepdims=False)
    visible = lax.dynamic_index_in_dim(visibility, tile_pos, 1, keepdims=True).astype(jnp.float32)
    padded_taps = jnp.pad(fir_taps, ((0, 0), (2 * LANES - TAPS, 0)))
    samp = gathered.shape[1]
    vmem = pl.BlockSpec(memory_space=pltpu.VMEM)
    smem = pl.BlockSpec(memory_space=pltpu.SMEM)
    windows = pl.pallas_call(
        window_kernel,
        out_shape=jax.ShapeDtypeStruct((sta, WLEN), jnp.float32),
        in_specs=[smem, smem, vmem, vmem, vmem],
        out_specs=vmem,
        scratch_shapes=[
            pltpu.VMEM((sta, samp + 2 * LANES), jnp.float32),
            pltpu.VMEM((sta, 4 * LANES), jnp.float32),
        ],
        compiler_params=pltpu.CompilerParams(vmem_limit_bytes=40 * 2**20),
        name="windows",
    )(begin_at, band_gain, gathered, padded_taps, visible)
    grid = delays.shape[1]
    block = grid // n
    image = pl.pallas_call(
        functools.partial(stack_kernel, n),
        out_shape=jax.ShapeDtypeStruct((L, block), jnp.float32),
        in_specs=[vmem, vmem],
        out_specs=vmem,
        scratch_shapes=[
            pltpu.VMEM((L, sta * D), jnp.bfloat16),
            pltpu.VMEM((L, block), jnp.float32),
            pltpu.VMEM((n - 1, L, block), jnp.bfloat16),
            pltpu.VMEM((n - 1, L, block), jnp.bfloat16),
            pltpu.SemaphoreType.DMA((n - 1,)),
            pltpu.SemaphoreType.DMA((n - 1,)),
        ],
        compiler_params=pltpu.CompilerParams(
            collective_id=0, has_side_effects=True, vmem_limit_bytes=48 * 2**20
        ),
        name="stack",
    )(delays, windows)
    lagged = jnp.flip(image.reshape(L // LANES, LANES, block), 1).reshape(L, block)
    return lagged.T


def solution(mesh):
    placed = (P("sta", "tile"), P(), P(), P("sta", None), P("sta", "tile"), P("sta", None))
    return jax.shard_map(
        on_device, mesh=mesh, in_specs=placed, out_specs=P(("tile", "sta"), None), check_vma=False
    )
```

profile of v0, /device:TPU:0, one launch (start us, length us, event | category | flops | bytes accessed | tf_op | source)
XLA Modules:
  0.0 85.8 jit_solution(16930862993044207633)
XLA Ops:
  0.0 0.0 copy-start
  0.0 0.0 copy-start.1
  0.0 0.7 copy-done
  0.7 0.7 constant_dynamic-slice_fusion
  1.4 0.8 pad.4.taps_ref
  2.1 0.1 copy.10
  2.3 9.2 %all_gather.3.traces_ref = bf16[192,1536]{1,0:T(8,128)(2,1)S(1)} all-gather(bf16[192,384]{1,0:T(8,128)(2,1)} %param.6), channel_id=1, replica_groups=mesh['sta'=8,'tile'=4] {'tile'}, dimensions={1}, use_global_device_ids=true | all-gather | bytes 737280 | tf_op jit(solution)/shard_map/all_gather | solution.py:160
  11.5 0.0 copy-start.2
  11.5 0.7 copy-done.2
  12.1 5.7 %windows.1.win_ref = f32[192,384]{1,0:T(8,128)S(1)} custom-call(s32[192]{0:T(256)S(1)} %bitcast.5, f32[4]{0:T(128)S(1)} %copy-done.2, bf16[192,1536]{1,0:T(8,128)(2,1)S(1)} %all_gather.3.traces_ref, f32[4,256]{1,0:T(4,128)S(1)} %pad.4.taps_ref, f32[192,1]{1,0:T(8,128)S(1)} %convert_element_type.5.vis_ref), custom_call_target="tpu_custom_call" | custom-call | tf_op jit(solution)/shard_map/windows/pallas_call | solution.py:167
  17.8 0.0 copy-done.1
  17.8 67.0 %stack.1 = f32[256,256]{1,0:T(8,128)S(1)} custom-call(s32[192,2048]{1,0:T(8,128)S(1)} %copy-done.1, f32[192,384]{1,0:T(8,128)S(1)} %windows.1.win_ref), custom_call_target="tpu_custom_call" | custom-call | tf_op jit(solution)/shard_map/stack/pallas_call | solution.py:181
  84.8 0.1 rev.4
  85.0 0.8 copy.9
  (2 shorter events, 0.0 us)
Async XLA Ops:
  0.0 0.7 copy-start
  0.0 17.8 %copy-start.1 = (s32[192,2048]{1,0:T(8,128)S(1)}, s32[192,2048]{1,0:T(8,128)}, u32[]{:S(2)}) copy-start(s32[192,2048]{1,0:T(8,128)} %delays_ref.1) | copy-start | bytes 4718596
  11.5 0.7 copy-start.2
where the time goes:
time: 86.1 us; the launch traced here: 85.8 us
  Pallas kernels  72.7 us (84%)
  blocking collectives  9.19 us (11%)
  local copies, waits for them, and re-layouts  3.89 us (5%)
    pallas_call x1, Pallas kernels, on_device(): pl.pallas_call(functools.partial(stack_kernel, n), out_shape=jax.ShapeDty...  67 us
    all_gather x1, blocking collectives, on_device(): gathered = lax.all_gather(traces, 'tile', axis=1, tiled=True)  9.19 us
    pallas_call x1, Pallas kernels, on_device(): pl.pallas_call(window_kernel, out_shape=jax.ShapeDtypeStruct((sta, WLEN),...  5.66 us

commit v1 on v0

--- a/solution.py
+++ b/solution.py
@@ -13,7 +13,7 @@
 L = 256
 WLEN = 384
 LANES = 128
-CHUNK = 8
+CHUNK = 32
 MESH = pl.DeviceIdType.MESH
 
 
@@ -44,17 +44,17 @@
         rest = table - high.astype(jnp.float32)
         mid = rest.astype(jnp.bfloat16)
         low = (rest - mid.astype(jnp.float32)).astype(jnp.bfloat16)
-        tables.append((high, mid, low))
+        tables.append(jnp.concatenate([low, mid, high], axis=0))
+    table = jnp.concatenate(tables, axis=1)
     parts = []
     for j in range(WLEN // LANES):
         x = held[:, j * LANES : (j + 2) * LANES].astype(jnp.bfloat16)
+        x = jnp.concatenate([x, x, x], axis=1)
+        filtered = jnp.dot(x, table, preferred_element_type=jnp.float32)
         total = None
         for b in range(bands):
-            filtered = None
-            for table in reversed(tables[b]):
-                term = jnp.dot(x, table, preferred_element_type=jnp.float32)
-                filtered = term if filtered is None else filtered + term
-            term = filtered * filtered * gain_ref[b]
+            band = filtered[:, b * LANES : (b + 1) * LANES]
+            term = band * band * gain_ref[b]
             total = term if total is None else total + term
         parts.append(total.astype(jnp.bfloat16).astype(jnp.float32))
     mean = sum(jnp.sum(part, axis=1, keepdims=True) for part in parts) / WLEN
@@ -80,20 +80,25 @@
 
     lax.fori_loop(1, n, greet, 0)
 
+    step = 16
+
     def build(i, carry):
         for k in range(CHUNK):
             s = i * CHUNK + k
-            rows = jnp.broadcast_to(win_ref[pl.ds(s, 1), :], (LANES, WLEN))
-            rows = pltpu.roll(rows, WLEN - (LANES - 1), 1, stride=1, stride_axis=0)
-            rows = rows[:, :L].astype(jnp.bfloat16)
+            rows = jnp.broadcast_to(win_ref[pl.ds(s, 1), :], (step, WLEN))
+            rows = pltpu.roll(rows, WLEN - (step - 1), 1, stride=1, stride_axis=0)
+            rows = rows.astype(jnp.bfloat16)
             at = pl.ds(pl.multiple_of(s * D, D), D)
-            for a in range(L // LANES):
-                hankel[a * LANES : (a + 1) * LANES, at] = rows[:, a * LANES : (a + 1) * LANES]
+            for m in range(LANES // step):
+                by = LANES - step - m * step
+                moved = pltpu.roll(rows, WLEN - by, 1) if by else rows
+                for a in range(L // LANES):
+                    first = a * LANES + m * step
+                    hankel[first : first + step, at] = moved[:, a * LANES : (a + 1) * LANES]
         return carry
 
     lax.fori_loop(0, sta // CHUNK, build, 0)
 
-    step = 16
     levels = [
         (lax.broadcasted_iota(jnp.int32, (step, block), 0) + k * step)
         .astype(jnp.float32)
@@ -111,14 +116,17 @@
             near = delays_ref[pl.ds(pl.multiple_of(c * CHUNK, CHUNK), CHUNK), columns].astype(
                 jnp.float32
             )
-            pieces = []
-            for k in range(CHUNK):
-                row = jnp.broadcast_to(near[k : k + 1, :], (step, block)).astype(jnp.bfloat16)
-                pieces.extend(jnp.where(row == level, one, zero) for level in levels)
-            onehot = jnp.concatenate(pieces, axis=0)
-            depth = CHUNK * D
-            lhs = hankel[:, pl.ds(pl.multiple_of(c * depth, depth), depth)]
-            total[...] += jnp.dot(lhs, onehot, preferred_element_type=jnp.float32)
+            sums = []
+            depth = CHUNK // 2 * D
+            for half in range(2):
+                pieces = []
+                for k in range(half * CHUNK // 2, (half + 1) * CHUNK // 2):
+                    row = jnp.broadcast_to(near[k : k + 1, :], (step, block)).astype(jnp.bfloat16)
+                    pieces.extend(jnp.where(row == level, one, zero) for level in levels)
+                onehot = jnp.concatenate(pieces, axis=0)
+                lhs = hankel[:, pl.ds(pl.multiple_of((2 * c + half) * depth, depth), depth)]
+                sums.append(jnp.dot(lhs, onehot, preferred_element_type=jnp.float32))
+            total[...] += sums[0] + sums[1]
             return carry
 
         lax.fori_loop(0, sta // CHUNK, add, 0)
@@ -137,12 +145,15 @@
 
     def send(o, carry):
         stack(lax.rem(me + o, n))
-        sent[o - 1] = total[...].astype(jnp.bfloat16)
-        copy_of(o).start()
-        return carry
-
-    lax.fori_loop(1, n, send, 0)
-    stack(me)
+
+        @pl.when(o < n)
+        def _():
+            sent[o - 1] = total[...].astype(jnp.bfloat16)
+            copy_of(o).start()
+
+        return carry
+
+    lax.fori_loop(1, n + 1, send, 0)
 
     def collect(o, carry):
         copy_of(o).wait()

time: 86.1 us -> 70.7 us (0.82)
  Pallas kernels: 72.7 us -> 57.3 us
    pallas_call x1, Pallas kernels: 67 us -> 53.1 us  [on_device(): pl.pallas_call(functools.partial(stack_kernel, n), out_shape=jax.ShapeDty...]
    pallas_call x1, Pallas kernels: 5.66 us -> 4.12 us  [on_device(): pl.pallas_call(window_kernel, out_shape=jax.ShapeDtypeStruct((sta, WLEN),...]
where the time goes in v1:
time: 70.7 us; the launch traced here: 70.4 us
  Pallas kernels  57.3 us (81%)
  blocking collectives  9.19 us (13%)
  local copies, waits for them, and re-layouts  3.89 us (6%)
    pallas_call x1, Pallas kernels, on_device(): pl.pallas_call(functools.partial(stack_kernel, n), out_shape=jax.ShapeDty...  53.1 us
    all_gather x1, blocking collectives, on_device(): gathered = lax.all_gather(traces, 'tile', axis=1, tiled=True)  9.19 us
    pallas_call x1, Pallas kernels, on_device(): pl.pallas_call(window_kernel, out_shape=jax.ShapeDtypeStruct((sta, WLEN),...  4.12 us
    unnamed x7, local copies, waits for them, and re-layouts  1.46 us

profile of v1, /device:TPU:0, one launch (start us, length us, event | category | flops | bytes accessed | tf_op | source)
XLA Modules:
  0.0 70.4 jit_solution(2460947054387836579)
XLA Ops:
  0.0 0.0 copy-start
  0.0 0.0 copy-start.1
  0.0 0.7 copy-done
  0.7 0.7 constant_dynamic-slice_fusion
  1.4 0.8 %pad.4.taps_ref = f32[4,256]{1,0:T(4,128)S(1)} pad(f32[4,64]{1,0:T(4,128)} %param.7, f32[]{:T(128)} %constant.16.clone.1), padding=0_0x192_0 | pad | bytes 5124 | tf_op jit(solution)/shard_map/jit(_pad)/pad | solution.py:174
  2.1 0.1 copy.10
  2.3 9.2 %all_gather.3.traces_ref = bf16[192,1536]{1,0:T(8,128)(2,1)S(1)} all-gather(bf16[192,384]{1,0:T(8,128)(2,1)} %param.6), channel_id=1, replica_groups=mesh['sta'=8,'tile'=4] {'tile'}, dimensions={1}, use_global_device_ids=true | all-gather | bytes 737280 | tf_op jit(solution)/shard_map/all_gather | solution.py:171
  11.5 0.0 copy-start.2
  11.5 0.7 copy-done.2
  12.1 4.1 %windows.1.win_ref = f32[192,384]{1,0:T(8,128)S(1)} custom-call(s32[192]{0:T(256)S(1)} %bitcast.5, f32[4]{0:T(128)S(1)} %copy-done.2, bf16[192,1536]{1,0:T(8,128)(2,1)S(1)} %all_gather.3.traces_ref, f32[4,256]{1,0:T(4,128)S(1)} %pad.4.taps_ref, f32[192,1]{1,0:T(8,128)S(1)} %convert_element_type.5.vis_ref), custom_call_target="tpu_custom_call" | custom-call | tf_op jit(solution)/shard_map/windows/pallas_call | solution.py:178
  16.3 0.0 copy-done.1
  16.3 53.1 %stack.1 = f32[256,256]{1,0:T(8,128)S(1)} custom-call(s32[192,2048]{1,0:T(8,128)S(1)} %copy-done.1, f32[192,384]{1,0:T(8,128)S(1)} %windows.1.win_ref), custom_call_target="tpu_custom_call" | custom-call | tf_op jit(solution)/shard_map/stack/pallas_call | solution.py:192
  69.4 0.1 rev.4
  69.6 0.8 %copy.9 = f32[256,256]{0,1:T(8,128)} copy(f32[256,256]{1,0:T(8,128)S(1)} %bitcast.6) | data formatting | bytes 524288 | tf_op jit(solution)/shard_map/reshape | solution.py:210
  (2 shorter events, 0.0 us)
Async XLA Ops:
  0.0 0.7 copy-start
  0.0 16.3 %copy-start.1 = (s32[192,2048]{1,0:T(8,128)S(1)}, s32[192,2048]{1,0:T(8,128)}, u32[]{:S(2)}) copy-start(s32[192,2048]{1,0:T(8,128)} %delays_ref.1) | copy-start | bytes 4718596
  11.5 0.7 copy-start.2

commit v2 on v1

--- a/solution.py
+++ b/solution.py
@@ -100,33 +100,33 @@
     lax.fori_loop(0, sta // CHUNK, build, 0)
 
     levels = [
-        (lax.broadcasted_iota(jnp.int32, (step, block), 0) + k * step)
+        (lax.broadcasted_iota(jnp.int32, (step, 2 * block), 0) + k * step)
         .astype(jnp.float32)
         .astype(jnp.bfloat16)
         for k in range(D // step)
     ]
-    one = jnp.ones((step, block), jnp.bfloat16)
-    zero = jnp.zeros((step, block), jnp.bfloat16)
-
-    def stack(owner):
-        columns = pl.ds(pl.multiple_of(owner * block, block), block)
+    one = jnp.ones((step, 2 * block), jnp.bfloat16)
+    zero = jnp.zeros((step, 2 * block), jnp.bfloat16)
+
+    def columns_of(o):
+        return pl.ds(pl.multiple_of(lax.rem(me + o, n) * block, block), block)
+
+    def stack(first, last):
         total[...] = jnp.zeros_like(total)
 
         def add(c, carry):
-            near = delays_ref[pl.ds(pl.multiple_of(c * CHUNK, CHUNK), CHUNK), columns].astype(
-                jnp.float32
-            )
-            sums = []
-            depth = CHUNK // 2 * D
-            for half in range(2):
-                pieces = []
-                for k in range(half * CHUNK // 2, (half + 1) * CHUNK // 2):
-                    row = jnp.broadcast_to(near[k : k + 1, :], (step, block)).astype(jnp.bfloat16)
-                    pieces.extend(jnp.where(row == level, one, zero) for level in levels)
-                onehot = jnp.concatenate(pieces, axis=0)
-                lhs = hankel[:, pl.ds(pl.multiple_of((2 * c + half) * depth, depth), depth)]
-                sums.append(jnp.dot(lhs, onehot, preferred_element_type=jnp.float32))
-            total[...] += sums[0] + sums[1]
+            rows = pl.ds(pl.multiple_of(c * CHUNK, CHUNK), CHUNK)
+            near = jnp.concatenate(
+                [delays_ref[rows, columns_of(first)], delays_ref[rows, columns_of(last)]], axis=1
+            ).astype(jnp.float32)
+            pieces = []
+            for k in range(CHUNK):
+                row = jnp.broadcast_to(near[k : k + 1, :], (step, 2 * block)).astype(jnp.bfloat16)
+                pieces.extend(jnp.where(row == level, one, zero) for level in levels)
+            onehot = jnp.concatenate(pieces, axis=0)
+            depth = CHUNK * D
+            lhs = hankel[:, pl.ds(pl.multiple_of(c * depth, depth), depth)]
+            total[...] += jnp.dot(lhs, onehot, preferred_element_type=jnp.float32)
             return carry
 
         lax.fori_loop(0, sta // CHUNK, add, 0)
@@ -143,25 +143,25 @@
 
     pl.semaphore_wait(barrier, n - 1)
 
-    def send(o, carry):
-        stack(lax.rem(me + o, n))
-
-        @pl.when(o < n)
+    def send(pair, carry):
+        o = 2 * pair + 1
+        stack(o, o + 1)
+        sent[o - 1] = total[:, :block].astype(jnp.bfloat16)
+        copy_of(o).start()
+
+        @pl.when(o + 1 < n)
         def _():
-            sent[o - 1] = total[...].astype(jnp.bfloat16)
-            copy_of(o).start()
-
-        return carry
-
-    lax.fori_loop(1, n + 1, send, 0)
-
-    def collect(o, carry):
+            sent[o] = total[:, block:].astype(jnp.bfloat16)
+            copy_of(o + 1).start()
+
+        return carry
+
+    lax.fori_loop(0, n // 2, send, 0)
+    image = total[:, block:]
+    for o in range(1, n):
         copy_of(o).wait()
-        total[...] += got[o - 1].astype(jnp.float32)
-        return carry
-
-    lax.fori_loop(1, n, collect, 0)
-    out_ref[...] = total[...] * (1.0 / math.sqrt(sta * n))
+        image += got[o - 1].astype(jnp.float32)
+    out_ref[...] = image * (1.0 / math.sqrt(sta * n))
 
 
 def on_device(traces, fir_taps, band_gain, starts, delays, visibility):
@@ -196,7 +196,7 @@
         out_specs=vmem,
         scratch_shapes=[
             pltpu.VMEM((L, sta * D), jnp.bfloat16),
-            pltpu.VMEM((L, block), jnp.float32),
+            pltpu.VMEM((L, 2 * block), jnp.float32),
             pltpu.VMEM((n - 1, L, block), jnp.bfloat16),
             pltpu.VMEM((n - 1, L, block), jnp.bfloat16),
             pltpu.SemaphoreType.DMA((n - 1,)),

time: 70.7 us -> 71.5 us (1.011)
  Pallas kernels: 57.3 us -> 58.1 us
    pallas_call x1, Pallas kernels: 53.1 us -> 53.9 us  [on_device(): pl.pallas_call(functools.partial(stack_kernel, n), out_shape=jax.ShapeDty...]
where the time goes in v2:
time: 71.5 us; the launch traced here: 71.2 us
  Pallas kernels  58.1 us (81%)
  blocking collectives  9.19 us (13%)
  local copies, waits for them, and re-layouts  3.89 us (5%)
    pallas_call x1, Pallas kernels, on_device(): pl.pallas_call(functools.partial(stack_kernel, n), out_shape=jax.ShapeDty...  53.9 us
    all_gather x1, blocking collectives, on_device(): gathered = lax.all_gather(traces, 'tile', axis=1, tiled=True)  9.19 us
    pallas_call x1, Pallas kernels, on_device(): pl.pallas_call(window_kernel, out_shape=jax.ShapeDtypeStruct((sta, WLEN),...  4.12 us
    unnamed x7, local copies, waits for them, and re-layouts  1.46 us

profile of v2, /device:TPU:0, one launch (start us, length us, event | category | flops | bytes accessed | tf_op | source)
XLA Modules:
  0.0 71.2 jit_solution(1436069924424853971)
XLA Ops:
  0.0 0.0 copy-start
  0.0 0.0 copy-start.1
  0.0 0.7 copy-done
  0.7 0.7 constant_dynamic-slice_fusion
  1.4 0.8 %pad.4.taps_ref = f32[4,256]{1,0:T(4,128)S(1)} pad(f32[4,64]{1,0:T(4,128)} %param.7, f32[]{:T(128)} %constant.16.clone.1), padding=0_0x192_0 | pad | bytes 5124 | tf_op jit(solution)/shard_map/jit(_pad)/pad | solution.py:174
  2.1 0.1 copy.10
  2.3 9.2 %all_gather.3.traces_ref = bf16[192,1536]{1,0:T(8,128)(2,1)S(1)} all-gather(bf16[192,384]{1,0:T(8,128)(2,1)} %param.6), channel_id=1, replica_groups=mesh['sta'=8,'tile'=4] {'tile'}, dimensions={1}, use_global_device_ids=true | all-gather | bytes 737280 | tf_op jit(solution)/shard_map/all_gather | solution.py:171
  11.5 0.0 copy-start.2
  11.5 0.7 copy-done.2
  12.1 4.1 %windows.1.win_ref = f32[192,384]{1,0:T(8,128)S(1)} custom-call(s32[192]{0:T(256)S(1)} %bitcast.5, f32[4]{0:T(128)S(1)} %copy-done.2, bf16[192,1536]{1,0:T(8,128)(2,1)S(1)} %all_gather.3.traces_ref, f32[4,256]{1,0:T(4,128)S(1)} %pad.4.taps_ref, f32[192,1]{1,0:T(8,128)S(1)} %convert_element_type.5.vis_ref), custom_call_target="tpu_custom_call" | custom-call | tf_op jit(solution)/shard_map/windows/pallas_call | solution.py:178
  16.3 0.0 copy-done.1
  16.3 53.9 %stack.1 = f32[256,256]{1,0:T(8,128)S(1)} custom-call(s32[192,2048]{1,0:T(8,128)S(1)} %copy-done.1, f32[192,384]{1,0:T(8,128)S(1)} %windows.1.win_ref), custom_call_target="tpu_custom_call" | custom-call | tf_op jit(solution)/shard_map/stack/pallas_call | solution.py:192
  70.2 0.1 rev.4
  70.4 0.8 %copy.9 = f32[256,256]{0,1:T(8,128)} copy(f32[256,256]{1,0:T(8,128)S(1)} %bitcast.6) | data formatting | bytes 524288 | tf_op jit(solution)/shard_map/reshape | solution.py:210
  (2 shorter events, 0.0 us)
Async XLA Ops:
  0.0 0.7 copy-start
  0.0 16.3 %copy-start.1 = (s32[192,2048]{1,0:T(8,128)S(1)}, s32[192,2048]{1,0:T(8,128)}, u32[]{:S(2)}) copy-start(s32[192,2048]{1,0:T(8,128)} %delays_ref.1) | copy-start | bytes 4718596
  11.5 0.7 copy-start.2

commit v3 on v1

--- a/solution.py
+++ b/solution.py
@@ -14,10 +14,11 @@
 WLEN = 384
 LANES = 128
 CHUNK = 32
+EIGHT = jnp.float8_e4m3fn
 MESH = pl.DeviceIdType.MESH
 
 
-def window_kernel(starts_ref, gain_ref, traces_ref, taps_ref, vis_ref, win_ref, padded, held):
+def window_kernel(starts_ref, gain_ref, traces_ref, taps_ref, vis_ref, win_ref, unit_ref, padded, held):
     sta, samp = traces_ref.shape
     bands = taps_ref.shape[0]
     padded[:, :LANES] = jnp.zeros((sta, LANES), jnp.float32)
@@ -59,12 +60,26 @@
         parts.append(total.astype(jnp.bfloat16).astype(jnp.float32))
     mean = sum(jnp.sum(part, axis=1, keepdims=True) for part in parts) / WLEN
     vis = vis_ref[...]
+    parts = [((part - mean) * vis).astype(jnp.bfloat16).astype(jnp.float32) for part in parts]
+    largest = functools.reduce(jnp.maximum, [jnp.max(jnp.abs(part), keepdims=True) for part in parts])
+    largest = largest * 2.0**-14
+    scale = jnp.full((1, 1), 2.0**-14, jnp.float32)
+    unit = jnp.full((1, 1), 2.0**14, jnp.float32)
+    for p in (64, 32, 16, 8, 4, 2, 1):
+        small = largest * 2.0**p < 256.0
+        largest = jnp.where(small, largest * 2.0**p, largest)
+        scale = jnp.where(small, scale * 2.0**p, scale)
+        unit = jnp.where(small, unit * 2.0**-p, unit)
+    unit_ref[...] = unit
     for j, part in enumerate(parts):
-        out = ((part - mean) * vis).astype(jnp.bfloat16)
-        win_ref[:, j * LANES : (j + 1) * LANES] = out.astype(jnp.float32)
-
-
-def stack_kernel(n, delays_ref, win_ref, out_ref, hankel, total, sent, got, send_sem, recv_sem):
+        scaled = part * scale
+        high = scaled.astype(EIGHT).astype(jnp.float32)
+        at = slice(j * LANES, (j + 1) * LANES)
+        win_ref[0, :, at] = high
+        win_ref[1, :, at] = (scaled - high) * 16.0
+
+
+def stack_kernel(n, delays_ref, win_ref, unit_ref, out_ref, hankel, total, sent, got, send_sem, recv_sem):
     sta = delays_ref.shape[0]
     block = out_ref.shape[1]
     me = lax.axis_index("sta")
@@ -80,24 +95,26 @@
 
     lax.fori_loop(1, n, greet, 0)
 
-    step = 16
+    step = 32
 
     def build(i, carry):
-        for k in range(CHUNK):
-            s = i * CHUNK + k
-            rows = jnp.broadcast_to(win_ref[pl.ds(s, 1), :], (step, WLEN))
-            rows = pltpu.roll(rows, WLEN - (step - 1), 1, stride=1, stride_axis=0)
-            rows = rows.astype(jnp.bfloat16)
+        for k in range(CHUNK // 2):
+            s = i * (CHUNK // 2) + k
             at = pl.ds(pl.multiple_of(s * D, D), D)
-            for m in range(LANES // step):
-                by = LANES - step - m * step
-                moved = pltpu.roll(rows, WLEN - by, 1) if by else rows
-                for a in range(L // LANES):
-                    first = a * LANES + m * step
-                    hankel[first : first + step, at] = moved[:, a * LANES : (a + 1) * LANES]
-        return carry
-
-    lax.fori_loop(0, sta // CHUNK, build, 0)
+            for term in range(2):
+                rows = jnp.broadcast_to(win_ref[term, pl.ds(s, 1), :], (step, WLEN))
+                rows = pltpu.roll(rows, WLEN - (step - 1), 1, stride=1, stride_axis=0)
+                rows = rows.astype(EIGHT)
+                for m in range(LANES // step):
+                    by = LANES - step - m * step
+                    moved = pltpu.roll(rows, WLEN - by, 1) if by else rows
+                    moved = moved[:, :L].astype(EIGHT)
+                    for a in range(L // LANES):
+                        first = term * L + a * LANES + m * step
+                        hankel[first : first + step, at] = moved[:, a * LANES : (a + 1) * LANES]
+        return carry
+
+    lax.fori_loop(0, sta // (CHUNK // 2), build, 0)
 
     levels = [
         (lax.broadcasted_iota(jnp.int32, (step, block), 0) + k * step)
@@ -107,6 +124,8 @@
     ]
     one = jnp.ones((step, block), jnp.bfloat16)
     zero = jnp.zeros((step, block), jnp.bfloat16)
+
+    unit = unit_ref[...]
 
     def stack(owner):
         columns = pl.ds(pl.multiple_of(owner * block, block), block)
@@ -122,11 +141,14 @@
                 pieces = []
                 for k in range(half * CHUNK // 2, (half + 1) * CHUNK // 2):
                     row = jnp.broadcast_to(near[k : k + 1, :], (step, block)).astype(jnp.bfloat16)
-                    pieces.extend(jnp.where(row == level, one, zero) for level in levels)
+                    pieces.extend(
+                        jnp.where(row == level, one, zero).astype(EIGHT) for level in levels
+                    )
                 onehot = jnp.concatenate(pieces, axis=0)
                 lhs = hankel[:, pl.ds(pl.multiple_of((2 * c + half) * depth, depth), depth)]
                 sums.append(jnp.dot(lhs, onehot, preferred_element_type=jnp.float32))
-            total[...] += sums[0] + sums[1]
+            both = sums[0] + sums[1]
+            total[...] += both[:L] + both[L:] * (1.0 / 16.0)
             return carry
 
         lax.fori_loop(0, sta // CHUNK, add, 0)
@@ -148,12 +170,13 @@
 
         @pl.when(o < n)
         def _():
-            sent[o - 1] = total[...].astype(jnp.bfloat16)
+            sent[o - 1] = (total[...] * unit).astype(jnp.bfloat16)
             copy_of(o).start()
 
         return carry
 
     lax.fori_loop(1, n + 1, send, 0)
+    total[...] *= unit
 
     def collect(o, carry):
         copy_of(o).wait()
@@ -175,11 +198,14 @@
     samp = gathered.shape[1]
     vmem = pl.BlockSpec(memory_space=pltpu.VMEM)
     smem = pl.BlockSpec(memory_space=pltpu.SMEM)
-    windows = pl.pallas_call(
+    windows, unit = pl.pallas_call(
         window_kernel,
-        out_shape=jax.ShapeDtypeStruct((sta, WLEN), jnp.float32),
+        out_shape=[
+            jax.ShapeDtypeStruct((2, sta, WLEN), jnp.float32),
+            jax.ShapeDtypeStruct((1, 1), jnp.float32),
+        ],
         in_specs=[smem, smem, vmem, vmem, vmem],
-        out_specs=vmem,
+        out_specs=[vmem, vmem],
         scratch_shapes=[
             pltpu.VMEM((sta, samp + 2 * LANES), jnp.float32),
             pltpu.VMEM((sta, 4 * LANES), jnp.float32),
@@ -192,10 +218,10 @@
     image = pl.pallas_call(
         functools.partial(stack_kernel, n),
         out_shape=jax.ShapeDtypeStruct((L, block), jnp.float32),
-        in_specs=[vmem, vmem],
+        in_specs=[vmem, vmem, vmem],
         out_specs=vmem,
         scratch_shapes=[
-            pltpu.VMEM((L, sta * D), jnp.bfloat16),
+            pltpu.VMEM((2 * L, sta * D), EIGHT),
             pltpu.VMEM((L, block), jnp.float32),
             pltpu.VMEM((n - 1, L, block), jnp.bfloat16),
             pltpu.VMEM((n - 1, L, block), jnp.bfloat16),
@@ -206,7 +232,7 @@
             collective_id=0, has_side_effects=True, vmem_limit_bytes=48 * 2**20
         ),
         name="stack",
-    )(delays, windows)
+    )(delays, windows, unit)
     lagged = jnp.flip(image.reshape(L // LANES, LANES, block), 1).reshape(L, block)
     return lagged.T
 

time: 70.7 us -> 85.8 us (1.21)
  Pallas kernels: 57.3 us -> 72.1 us
    pallas_call x1, Pallas kernels: 53.1 us -> 67.4 us  [on_device(): pl.pallas_call(functools.partial(stack_kernel, n), out_shape=jax.ShapeDty...]
where the time goes in v3:
time: 85.8 us; the launch traced here: 85.3 us
  Pallas kernels  72.1 us (84%)
  blocking collectives  9.19 us (11%)
  local copies, waits for them, and re-layouts  3.89 us (5%)
    pallas_call x1, Pallas kernels, on_device(): pl.pallas_call(functools.partial(stack_kernel, n), out_shape=jax.ShapeDty...  67.4 us
    all_gather x1, blocking collectives, on_device(): gathered = lax.all_gather(traces, 'tile', axis=1, tiled=True)  9.19 us
    pallas_call x1, Pallas kernels, on_device(): pl.pallas_call(window_kernel, out_shape=[jax.ShapeDtypeStruct((2, sta, WL...  4.78 us

profile of v3, /device:TPU:0, one launch (start us, length us, event | category | flops | bytes accessed | tf_op | source)
XLA Modules:
  0.0 85.3 jit_solution(10481038058186728503)
XLA Ops:
  0.0 0.0 copy-start
  0.0 0.0 copy-start.1
  0.0 0.7 copy-done
  0.7 0.7 constant_dynamic-slice_fusion
  1.4 0.8 pad.4.taps_ref
  2.1 0.1 copy.10
  2.3 9.2 %all_gather.3.traces_ref = bf16[192,1536]{1,0:T(8,128)(2,1)S(1)} all-gather(bf16[192,384]{1,0:T(8,128)(2,1)} %param.6), channel_id=1, replica_groups=mesh['sta'=8,'tile'=4] {'tile'}, dimensions={1}, use_global_device_ids=true | all-gather | bytes 737280 | tf_op jit(solution)/shard_map/all_gather | solution.py:194
  11.5 0.0 copy-start.2
  11.5 0.7 copy-done.2
  12.1 4.8 %windows.1 = (f32[2,192,384]{2,1,0:T(8,128)S(1)}, f32[1,1]{1,0:T(1,128)}) custom-call(s32[192]{0:T(256)S(1)} %bitcast.5, f32[4]{0:T(128)S(1)} %copy-done.2, bf16[192,1536]{1,0:T(8,128)(2,1)S(1)} %all_gather.3.traces_ref, f32[4,256]{1,0:T(4,128)S(1)} %pad.4.taps_ref, f32[192,1]{1,0:T(8,128)S(1)} %convert_element_type.5.vis_ref), custom_call_target="tpu_custom_call" | custom-call | tf_op jit(solution)/shard_map/windows/pallas_call | solution.py:201
  16.9 0.0 copy-done.1
  16.9 67.4 %stack.1 = f32[256,256]{1,0:T(8,128)S(1)} custom-call(s32[192,2048]{1,0:T(8,128)S(1)} %copy-done.1, f32[2,192,384]{2,1,0:T(8,128)S(1)} %get-tuple-element.7.win_ref, f32[1,1]{1,0:T(1,128)} %get-tuple-element.8.unit_ref), custom_call_target="tpu_custom_call" | custom-call | tf_op jit(solution)/shard_map/stack/pallas_call | solution.py:218
  84.3 0.1 rev.4
  84.4 0.8 copy.9
  (2 shorter events, 0.0 us)
Async XLA Ops:
  0.0 0.7 copy-start
  0.0 16.9 %copy-start.1 = (s32[192,2048]{1,0:T(8,128)S(1)}, s32[192,2048]{1,0:T(8,128)}, u32[]{:S(2)}) copy-start(s32[192,2048]{1,0:T(8,128)} %delays_ref.1) | copy-start | bytes 4718596
  11.5 0.7 copy-start.2

commit v4 on v1

--- a/solution.py
+++ b/solution.py
@@ -99,30 +99,21 @@
 
     lax.fori_loop(0, sta // CHUNK, build, 0)
 
-    levels = [
-        (lax.broadcasted_iota(jnp.int32, (step, block), 0) + k * step)
-        .astype(jnp.float32)
-        .astype(jnp.bfloat16)
-        for k in range(D // step)
-    ]
-    one = jnp.ones((step, block), jnp.bfloat16)
-    zero = jnp.zeros((step, block), jnp.bfloat16)
+    level = lax.broadcasted_iota(jnp.int32, (D, block), 0)
 
     def stack(owner):
         columns = pl.ds(pl.multiple_of(owner * block, block), block)
         total[...] = jnp.zeros_like(total)
 
         def add(c, carry):
-            near = delays_ref[pl.ds(pl.multiple_of(c * CHUNK, CHUNK), CHUNK), columns].astype(
-                jnp.float32
-            )
+            near = delays_ref[pl.ds(pl.multiple_of(c * CHUNK, CHUNK), CHUNK), columns]
             sums = []
             depth = CHUNK // 2 * D
             for half in range(2):
                 pieces = []
                 for k in range(half * CHUNK // 2, (half + 1) * CHUNK // 2):
-                    row = jnp.broadcast_to(near[k : k + 1, :], (step, block)).astype(jnp.bfloat16)
-                    pieces.extend(jnp.where(row == level, one, zero) for level in levels)
+                    row = jnp.broadcast_to(near[k : k + 1, :], (D, block))
+                    pieces.append(jnp.where(row == level, 1.0, 0.0).astype(jnp.bfloat16))
                 onehot = jnp.concatenate(pieces, axis=0)
                 lhs = hankel[:, pl.ds(pl.multiple_of((2 * c + half) * depth, depth), depth)]
                 sums.append(jnp.dot(lhs, onehot, preferred_element_type=jnp.float32))

time: 70.7 us -> 71 us (level)
  no operation moved by 1% of the time
where the time goes in v4:
time: 71 us; the launch traced here: 70.8 us
  Pallas kernels  57.6 us (81%)
  blocking collectives  9.19 us (13%)
  local copies, waits for them, and re-layouts  3.89 us (5%)
    pallas_call x1, Pallas kernels, on_device(): pl.pallas_call(functools.partial(stack_kernel, n), out_shape=jax.ShapeDty...  53.5 us
    all_gather x1, blocking collectives, on_device(): gathered = lax.all_gather(traces, 'tile', axis=1, tiled=True)  9.19 us
    pallas_call x1, Pallas kernels, on_device(): pl.pallas_call(window_kernel, out_shape=jax.ShapeDtypeStruct((sta, WLEN),...  4.12 us
    unnamed x7, local copies, waits for them, and re-layouts  1.46 us

profile of v4, /device:TPU:0, one launch (start us, length us, event | category | flops | bytes accessed | tf_op | source)
XLA Modules:
  0.0 70.8 jit_solution(8577942479379774602)
XLA Ops:
  0.0 0.0 copy-start
  0.0 0.0 copy-start.1
  0.0 0.7 copy-done
  0.7 0.7 constant_dynamic-slice_fusion
  1.4 0.8 %pad.4.taps_ref = f32[4,256]{1,0:T(4,128)S(1)} pad(f32[4,64]{1,0:T(4,128)} %param.7, f32[]{:T(128)} %constant.16.clone.1), padding=0_0x192_0 | pad | bytes 5124 | tf_op jit(solution)/shard_map/jit(_pad)/pad | solution.py:165
  2.1 0.1 copy.10
  2.3 9.2 %all_gather.3.traces_ref = bf16[192,1536]{1,0:T(8,128)(2,1)S(1)} all-gather(bf16[192,384]{1,0:T(8,128)(2,1)} %param.6), channel_id=1, replica_groups=mesh['sta'=8,'tile'=4] {'tile'}, dimensions={1}, use_global_device_ids=true | all-gather | bytes 737280 | tf_op jit(solution)/shard_map/all_gather | solution.py:162
  11.5 0.0 copy-start.2
  11.5 0.7 copy-done.2
  12.1 4.1 %windows.1.win_ref = f32[192,384]{1,0:T(8,128)S(1)} custom-call(s32[192]{0:T(256)S(1)} %bitcast.5, f32[4]{0:T(128)S(1)} %copy-done.2, bf16[192,1536]{1,0:T(8,128)(2,1)S(1)} %all_gather.3.traces_ref, f32[4,256]{1,0:T(4,128)S(1)} %pad.4.taps_ref, f32[192,1]{1,0:T(8,128)S(1)} %convert_element_type.5.vis_ref), custom_call_target="tpu_custom_call" | custom-call | tf_op jit(solution)/shard_map/windows/pallas_call | solution.py:169
  16.3 0.0 copy-done.1
  16.3 53.5 %stack.1 = f32[256,256]{1,0:T(8,128)S(1)} custom-call(s32[192,2048]{1,0:T(8,128)S(1)} %copy-done.1, f32[192,384]{1,0:T(8,128)S(1)} %windows.1.win_ref), custom_call_target="tpu_custom_call" | custom-call | tf_op jit(solution)/shard_map/stack/pallas_call | solution.py:183
  69.8 0.1 rev.4
  69.9 0.8 %copy.9 = f32[256,256]{0,1:T(8,128)} copy(f32[256,256]{1,0:T(8,128)S(1)} %bitcast.6) | data formatting | bytes 524288 | tf_op jit(solution)/shard_map/reshape | solution.py:201
  (2 shorter events, 0.0 us)
Async XLA Ops:
  0.0 0.7 copy-start
  0.0 16.3 %copy-start.1 = (s32[192,2048]{1,0:T(8,128)S(1)}, s32[192,2048]{1,0:T(8,128)}, u32[]{:S(2)}) copy-start(s32[192,2048]{1,0:T(8,128)} %delays_ref.1) | copy-start | bytes 4718596
  11.5 0.7 copy-start.2

commit v5 on v2

--- a/solution.py
+++ b/solution.py
@@ -13,7 +13,7 @@
 L = 256
 WLEN = 384
 LANES = 128
-CHUNK = 32
+CHUNK = 16
 MESH = pl.DeviceIdType.MESH
 
 
@@ -66,7 +66,7 @@
 
 def stack_kernel(n, delays_ref, win_ref, out_ref, hankel, total, sent, got, send_sem, recv_sem):
     sta = delays_ref.shape[0]
-    block = out_ref.shape[1]
+    block = out_ref.shape[0]
     me = lax.axis_index("sta")
     tile = lax.axis_index("tile")
 
@@ -88,25 +88,16 @@
             rows = jnp.broadcast_to(win_ref[pl.ds(s, 1), :], (step, WLEN))
             rows = pltpu.roll(rows, WLEN - (step - 1), 1, stride=1, stride_axis=0)
             rows = rows.astype(jnp.bfloat16)
-            at = pl.ds(pl.multiple_of(s * D, D), D)
             for m in range(LANES // step):
                 by = LANES - step - m * step
                 moved = pltpu.roll(rows, WLEN - by, 1) if by else rows
-                for a in range(L // LANES):
-                    first = a * LANES + m * step
-                    hankel[first : first + step, at] = moved[:, a * LANES : (a + 1) * LANES]
+                at = pl.ds(pl.multiple_of(s * D + m * step, step), step)
+                hankel[at, :] = moved[:, :L]
         return carry
 
     lax.fori_loop(0, sta // CHUNK, build, 0)
 
-    levels = [
-        (lax.broadcasted_iota(jnp.int32, (step, 2 * block), 0) + k * step)
-        .astype(jnp.float32)
-        .astype(jnp.bfloat16)
-        for k in range(D // step)
-    ]
-    one = jnp.ones((step, 2 * block), jnp.bfloat16)
-    zero = jnp.zeros((step, 2 * block), jnp.bfloat16)
+    level = D - 1 - lax.broadcasted_iota(jnp.int32, (2 * block, D), 1)
 
     def columns_of(o):
         return pl.ds(pl.multiple_of(lax.rem(me + o, n) * block, block), block)
@@ -117,16 +108,17 @@
         def add(c, carry):
             rows = pl.ds(pl.multiple_of(c * CHUNK, CHUNK), CHUNK)
             near = jnp.concatenate(
-                [delays_ref[rows, columns_of(first)], delays_ref[rows, columns_of(last)]], axis=1
-            ).astype(jnp.float32)
+                [delays_ref[rows, columns_of(first)].T, delays_ref[rows, columns_of(last)].T],
+                axis=0,
+            )
             pieces = []
             for k in range(CHUNK):
-                row = jnp.broadcast_to(near[k : k + 1, :], (step, 2 * block)).astype(jnp.bfloat16)
-                pieces.extend(jnp.where(row == level, one, zero) for level in levels)
-            onehot = jnp.concatenate(pieces, axis=0)
+                column = jnp.broadcast_to(near[:, k : k + 1], (2 * block, D))
+                pieces.append(jnp.where(column == level, 1.0, 0.0).astype(jnp.bfloat16))
+            onehot = jnp.concatenate(pieces, axis=1)
             depth = CHUNK * D
-            lhs = hankel[:, pl.ds(pl.multiple_of(c * depth, depth), depth)]
-            total[...] += jnp.dot(lhs, onehot, preferred_element_type=jnp.float32)
+            rhs = hankel[pl.ds(pl.multiple_of(c * depth, depth), depth), :]
+            total[...] += jnp.dot(onehot, rhs, preferred_element_type=jnp.float32)
             return carry
 
         lax.fori_loop(0, sta // CHUNK, add, 0)
@@ -146,18 +138,18 @@
     def send(pair, carry):
         o = 2 * pair + 1
         stack(o, o + 1)
-        sent[o - 1] = total[:, :block].astype(jnp.bfloat16)
+        sent[o - 1] = total[:block, :].astype(jnp.bfloat16)
         copy_of(o).start()
 
         @pl.when(o + 1 < n)
         def _():
-            sent[o] = total[:, block:].astype(jnp.bfloat16)
+            sent[o] = total[block:, :].astype(jnp.bfloat16)
             copy_of(o + 1).start()
 
         return carry
 
     lax.fori_loop(0, n // 2, send, 0)
-    image = total[:, block:]
+    image = total[block:, :]
     for o in range(1, n):
         copy_of(o).wait()
         image += got[o - 1].astype(jnp.float32)
@@ -189,16 +181,16 @@
     )(begin_at, band_gain, gathered, padded_taps, visible)
     grid = delays.shape[1]
     block = grid // n
-    image = pl.pallas_call(
+    return pl.pallas_call(
         functools.partial(stack_kernel, n),
-        out_shape=jax.ShapeDtypeStruct((L, block), jnp.float32),
+        out_shape=jax.ShapeDtypeStruct((block, L), jnp.float32),
         in_specs=[vmem, vmem],
         out_specs=vmem,
         scratch_shapes=[
-            pltpu.VMEM((L, sta * D), jnp.bfloat16),
-            pltpu.VMEM((L, 2 * block), jnp.float32),
-            pltpu.VMEM((n - 1, L, block), jnp.bfloat16),
-            pltpu.VMEM((n - 1, L, block), jnp.bfloat16),
+            pltpu.VMEM((sta * D, L), jnp.bfloat16),
+            pltpu.VMEM((2 * block, L), jnp.float32),
+            pltpu.VMEM((n - 1, block, L), jnp.bfloat16),
+            pltpu.VMEM((n - 1, block, L), jnp.bfloat16),
             pltpu.SemaphoreType.DMA((n - 1,)),
             pltpu.SemaphoreType.DMA((n - 1,)),
         ],
@@ -207,8 +199,6 @@
         ),
         name="stack",
     )(delays, windows)
-    lagged = jnp.flip(image.reshape(L // LANES, LANES, block), 1).reshape(L, block)
-    return lagged.T
 
 
 def solution(mesh):

time: 71.5 us -> 110 us (1.54)
  Pallas kernels: 58.1 us -> 96.5 us
    pallas_call x1, Pallas kernels: 53.9 us -> 92.1 us  [on_device(): pl.pallas_call(functools.partial(stack_kernel, n), out_shape=jax.ShapeDty...]
where the time goes in v5:
time: 110 us; the launch traced here: 109 us
  Pallas kernels  96.5 us (88%)
  blocking collectives  9.19 us (8%)
  local copies, waits for them, and re-layouts  3.61 us (3%)
    pallas_call x1, Pallas kernels, on_device(): pl.pallas_call(functools.partial(stack_kernel, n), out_shape=jax.ShapeDty...  92.1 us
    all_gather x1, blocking collectives, on_device(): gathered = lax.all_gather(traces, 'tile', axis=1, tiled=True)  9.19 us
    pallas_call x1, Pallas kernels, on_device(): pl.pallas_call(window_kernel, out_shape=jax.ShapeDtypeStruct((sta, WLEN),...  4.45 us

profile of v5, /device:TPU:0, one launch (start us, length us, event | category | flops | bytes accessed | tf_op | source)
XLA Modules:
  0.0 109.4 jit_solution(8101461751019083984)
XLA Ops:
  0.0 0.0 copy-start
  0.0 0.0 copy-start.1
  0.0 0.7 copy-done
  0.7 0.7 constant_dynamic-slice_fusion
  1.4 0.8 pad.4.taps_ref
  2.1 0.1 copy.8
  2.3 9.2 %all_gather.3.traces_ref = bf16[192,1536]{1,0:T(8,128)(2,1)S(1)} all-gather(bf16[192,384]{1,0:T(8,128)(2,1)} %param.6), channel_id=1, replica_groups=mesh['sta'=8,'tile'=4] {'tile'}, dimensions={1}, use_global_device_ids=true | all-gather | bytes 737280 | tf_op jit(solution)/shard_map/all_gather | solution.py:163
  11.5 0.0 copy-start.2
  11.5 0.7 copy-done.2
  12.1 4.5 %windows.1.win_ref = f32[192,384]{1,0:T(8,128)S(1)} custom-call(s32[192]{0:T(256)S(1)} %bitcast.1, f32[4]{0:T(128)S(1)} %copy-done.2, bf16[192,1536]{1,0:T(8,128)(2,1)S(1)} %all_gather.3.traces_ref, f32[4,256]{1,0:T(4,128)S(1)} %pad.4.taps_ref, f32[192,1]{1,0:T(8,128)S(1)} %convert_element_type.5.vis_ref), custom_call_target="tpu_custom_call" | custom-call | tf_op jit(solution)/shard_map/windows/pallas_call | solution.py:170
  16.6 0.0 copy-done.1
  16.6 92.1 %stack.1 = f32[256,256]{1,0:T(8,128)S(1)} custom-call(s32[192,2048]{1,0:T(8,128)S(1)} %copy-done.1, f32[192,384]{1,0:T(8,128)S(1)} %windows.1.win_ref), custom_call_target="tpu_custom_call" | custom-call | tf_op jit(solution)/shard_map/stack/pallas_call | solution.py:184
  108.7 0.7 copy.10
  (2 shorter events, 0.0 us)
Async XLA Ops:
  0.0 0.7 copy-start
  0.0 16.6 %copy-start.1 = (s32[192,2048]{1,0:T(8,128)S(1)}, s32[192,2048]{1,0:T(8,128)}, u32[]{:S(2)}) copy-start(s32[192,2048]{1,0:T(8,128)} %delays_ref.1) | copy-start | bytes 4718596
  11.5 0.7 copy-start.2

commit v6 on v3

--- a/solution.py
+++ b/solution.py
@@ -117,13 +117,11 @@
     lax.fori_loop(0, sta // (CHUNK // 2), build, 0)
 
     levels = [
-        (lax.broadcasted_iota(jnp.int32, (step, block), 0) + k * step)
-        .astype(jnp.float32)
-        .astype(jnp.bfloat16)
+        (lax.broadcasted_iota(jnp.int32, (step, block), 0) + k * step).astype(jnp.int8)
         for k in range(D // step)
     ]
-    one = jnp.ones((step, block), jnp.bfloat16)
-    zero = jnp.zeros((step, block), jnp.bfloat16)
+    one = jnp.ones((step, block), EIGHT)
+    zero = jnp.zeros((step, block), EIGHT)
 
     unit = unit_ref[...]
 
@@ -132,18 +130,14 @@
         total[...] = jnp.zeros_like(total)
 
         def add(c, carry):
-            near = delays_ref[pl.ds(pl.multiple_of(c * CHUNK, CHUNK), CHUNK), columns].astype(
-                jnp.float32
-            )
+            near = delays_ref[pl.ds(pl.multiple_of(c * CHUNK, CHUNK), CHUNK), columns]
             sums = []
             depth = CHUNK // 2 * D
             for half in range(2):
                 pieces = []
                 for k in range(half * CHUNK // 2, (half + 1) * CHUNK // 2):
-                    row = jnp.broadcast_to(near[k : k + 1, :], (step, block)).astype(jnp.bfloat16)
-                    pieces.extend(
-                        jnp.where(row == level, one, zero).astype(EIGHT) for level in levels
-                    )
+                    row = jnp.broadcast_to(near[k : k + 1, :], (step, block)).astype(jnp.int8)
+                    pieces.extend(jnp.where(row == level, one, zero) for level in levels)
                 onehot = jnp.concatenate(pieces, axis=0)
                 lhs = hankel[:, pl.ds(pl.multiple_of((2 * c + half) * depth, depth), depth)]
                 sums.append(jnp.dot(lhs, onehot, preferred_element_type=jnp.float32))

time: 85.8 us -> 85.6 us (level)
  no operation moved by 1% of the time
where the time goes in v6:
time: 85.6 us; the launch traced here: 85 us
  Pallas kernels  71.9 us (84%)
  blocking collectives  9.19 us (11%)
  local copies, waits for them, and re-layouts  3.89 us (5%)
    pallas_call x1, Pallas kernels, on_device(): pl.pallas_call(functools.partial(stack_kernel, n), out_shape=jax.ShapeDty...  67.1 us
    all_gather x1, blocking collectives, on_device(): gathered = lax.all_gather(traces, 'tile', axis=1, tiled=True)  9.19 us
    pallas_call x1, Pallas kernels, on_device(): pl.pallas_call(window_kernel, out_shape=[jax.ShapeDtypeStruct((2, sta, WL...  4.78 us

profile of v6, /device:TPU:0, one launch (start us, length us, event | category | flops | bytes accessed | tf_op | source)
XLA Modules:
  0.0 85.0 jit_solution(12843892274468454999)
XLA Ops:
  0.0 0.0 copy-start
  0.0 0.0 copy-start.1
  0.0 0.7 copy-done
  0.7 0.7 constant_dynamic-slice_fusion
  1.4 0.8 pad.4.taps_ref
  2.1 0.1 copy.10
  2.3 9.2 %all_gather.3.traces_ref = bf16[192,1536]{1,0:T(8,128)(2,1)S(1)} all-gather(bf16[192,384]{1,0:T(8,128)(2,1)} %param.6), channel_id=1, replica_groups=mesh['sta'=8,'tile'=4] {'tile'}, dimensions={1}, use_global_device_ids=true | all-gather | bytes 737280 | tf_op jit(solution)/shard_map/all_gather | solution.py:188
  11.5 0.0 copy-start.2
  11.5 0.7 copy-done.2
  12.1 4.8 %windows.1 = (f32[2,192,384]{2,1,0:T(8,128)S(1)}, f32[1,1]{1,0:T(1,128)}) custom-call(s32[192]{0:T(256)S(1)} %bitcast.5, f32[4]{0:T(128)S(1)} %copy-done.2, bf16[192,1536]{1,0:T(8,128)(2,1)S(1)} %all_gather.3.traces_ref, f32[4,256]{1,0:T(4,128)S(1)} %pad.4.taps_ref, f32[192,1]{1,0:T(8,128)S(1)} %convert_element_type.5.vis_ref), custom_call_target="tpu_custom_call" | custom-call | tf_op jit(solution)/shard_map/windows/pallas_call | solution.py:195
  16.9 0.0 copy-done.1
  16.9 67.1 %stack.1 = f32[256,256]{1,0:T(8,128)S(1)} custom-call(s32[192,2048]{1,0:T(8,128)S(1)} %copy-done.1, f32[2,192,384]{2,1,0:T(8,128)S(1)} %get-tuple-element.7.win_ref, f32[1,1]{1,0:T(1,128)} %get-tuple-element.8.unit_ref), custom_call_target="tpu_custom_call" | custom-call | tf_op jit(solution)/shard_map/stack/pallas_call | solution.py:212
  84.0 0.1 rev.4
  84.2 0.8 copy.9
  (2 shorter events, 0.0 us)
Async XLA Ops:
  0.0 0.7 copy-start
  0.0 16.9 %copy-start.1 = (s32[192,2048]{1,0:T(8,128)S(1)}, s32[192,2048]{1,0:T(8,128)}, u32[]{:S(2)}) copy-start(s32[192,2048]{1,0:T(8,128)} %delays_ref.1) | copy-start | bytes 4718596
  11.5 0.7 copy-start.2

commit v7 on v1

--- a/solution.py
+++ b/solution.py
@@ -81,6 +81,7 @@
     lax.fori_loop(1, n, greet, 0)
 
     step = 16
+    lane = lax.broadcasted_iota(jnp.int32, (step, LANES), 1)
 
     def build(i, carry):
         for k in range(CHUNK):
@@ -91,10 +92,15 @@
             at = pl.ds(pl.multiple_of(s * D, D), D)
             for m in range(LANES // step):
                 by = LANES - step - m * step
-                moved = pltpu.roll(rows, WLEN - by, 1) if by else rows
+                moved = [rows[:, c * LANES : (c + 1) * LANES] for c in range(WLEN // LANES)]
+                if by:
+                    moved = [pltpu.roll(part, LANES - by, 1) for part in moved]
                 for a in range(L // LANES):
                     first = a * LANES + m * step
-                    hankel[first : first + step, at] = moved[:, a * LANES : (a + 1) * LANES]
+                    part = moved[a]
+                    if by:
+                        part = jnp.where(lane < LANES - by, part, moved[a + 1])
+                    hankel[first : first + step, at] = part
         return carry
 
     lax.fori_loop(0, sta // CHUNK, build, 0)

time: 70.7 us -> 70.7 us (level)
  no operation moved by 1% of the time
where the time goes in v7:
time: 70.7 us; the launch traced here: 70.4 us
  Pallas kernels  57.3 us (81%)
  blocking collectives  9.19 us (13%)
  local copies, waits for them, and re-layouts  3.89 us (6%)
    pallas_call x1, Pallas kernels, on_device(): pl.pallas_call(functools.partial(stack_kernel, n), out_shape=jax.ShapeDty...  53.1 us
    all_gather x1, blocking collectives, on_device(): gathered = lax.all_gather(traces, 'tile', axis=1, tiled=True)  9.19 us
    pallas_call x1, Pallas kernels, on_device(): pl.pallas_call(window_kernel, out_shape=jax.ShapeDtypeStruct((sta, WLEN),...  4.12 us
    unnamed x7, local copies, waits for them, and re-layouts  1.46 us

profile of v7, /device:TPU:0, one launch (start us, length us, event | category | flops | bytes accessed | tf_op | source)
XLA Modules:
  0.0 70.4 jit_solution(17505655564546294994)
XLA Ops:
  0.0 0.0 copy-start
  0.0 0.0 copy-start.1
  0.0 0.7 copy-done
  0.7 0.7 constant_dynamic-slice_fusion
  1.4 0.8 %pad.4.taps_ref = f32[4,256]{1,0:T(4,128)S(1)} pad(f32[4,64]{1,0:T(4,128)} %param.7, f32[]{:T(128)} %constant.16.clone.1), padding=0_0x192_0 | pad | bytes 5124 | tf_op jit(solution)/shard_map/jit(_pad)/pad | solution.py:180
  2.1 0.1 copy.10
  2.3 9.2 %all_gather.3.traces_ref = bf16[192,1536]{1,0:T(8,128)(2,1)S(1)} all-gather(bf16[192,384]{1,0:T(8,128)(2,1)} %param.6), channel_id=1, replica_groups=mesh['sta'=8,'tile'=4] {'tile'}, dimensions={1}, use_global_device_ids=true | all-gather | bytes 737280 | tf_op jit(solution)/shard_map/all_gather | solution.py:177
  11.5 0.0 copy-start.2
  11.5 0.7 copy-done.2
  12.1 4.1 %windows.1.win_ref = f32[192,384]{1,0:T(8,128)S(1)} custom-call(s32[192]{0:T(256)S(1)} %bitcast.5, f32[4]{0:T(128)S(1)} %copy-done.2, bf16[192,1536]{1,0:T(8,128)(2,1)S(1)} %all_gather.3.traces_ref, f32[4,256]{1,0:T(4,128)S(1)} %pad.4.taps_ref, f32[192,1]{1,0:T(8,128)S(1)} %convert_element_type.5.vis_ref), custom_call_target="tpu_custom_call" | custom-call | tf_op jit(solution)/shard_map/windows/pallas_call | solution.py:184
  16.3 0.0 copy-done.1
  16.3 53.1 %stack.1 = f32[256,256]{1,0:T(8,128)S(1)} custom-call(s32[192,2048]{1,0:T(8,128)S(1)} %copy-done.1, f32[192,384]{1,0:T(8,128)S(1)} %windows.1.win_ref), custom_call_target="tpu_custom_call" | custom-call | tf_op jit(solution)/shard_map/stack/pallas_call | solution.py:198
  69.4 0.1 rev.4
  69.6 0.8 %copy.9 = f32[256,256]{0,1:T(8,128)} copy(f32[256,256]{1,0:T(8,128)S(1)} %bitcast.6) | data formatting | bytes 524288 | tf_op jit(solution)/shard_map/reshape | solution.py:216
  (2 shorter events, 0.0 us)
Async XLA Ops:
  0.0 0.7 copy-start
  0.0 16.3 %copy-start.1 = (s32[192,2048]{1,0:T(8,128)S(1)}, s32[192,2048]{1,0:T(8,128)}, u32[]{:S(2)}) copy-start(s32[192,2048]{1,0:T(8,128)} %delays_ref.1) | copy-start | bytes 4718596
  11.5 0.7 copy-start.2
